TPU v7x, 32 devices: a whole 2x2x4 slice. The times are simulated.
32 devices in a mesh: atoms: 16 (over z, x, core), width: 2 (over y).
Axes of the slice: x: 2, y: 2, z: 4, core: 2. Of those that a mesh axis runs over, the one named last changes fastest.
Arguments:
- tokens: bfloat16 [2048, 8192], P('atoms', 'width'), may hold values from -6 to 6
- dec_bias: float32 [8192], P('width'), may hold values from -3 to 3
- encoder: bfloat16 [2048, 8192], P('atoms', 'width'), may hold values from -1.5 to 1.5
- enc_bias: float32 [2048], P('atoms'), may hold values from -24 to 24
- decoder: bfloat16 [2048, 8192], P('atoms', 'width'), may hold values from -0.25 to 0.25
- atom_ids: int32 [2048, 16], P('atoms'), may hold values from 0 to 2047, as said below
- block_count: int32 [16], P('atoms'), may hold values from 1 to 2, as said below
Outputs:
- residual: bfloat16 [2048, 8192], P('atoms', 'width')
- encoder_grad: bfloat16 [2048, 8192], P('atoms', 'width')
- decoder_grad: bfloat16 [2048, 8192], P('atoms', 'width')
- bias_grad: float32 [2048], P('atoms')
Inputs may be any that keep to these rules, and one draw needn't show every extreme that they name: atom_ids[t, 2g] and atom_ids[t, 2g + 1] are two different atom slots of one owner o (slot // 128 = o), both below o * 128 + 64 block_count[o]; the 8 owners of one token differ. Of the 128 tokens of one index of atoms, at most 96 use any one owner, and in every draw some owner is used by exactly 96 tokens of every index of atoms. `block_count`: every draw has an owner with 2 live blocks and one with a single live block.
All inputs are finite; a program needn't handle non-finite values.
Results may differ from a plain program's by a relative error of at most 0.018.
Values may be sent and summed in bfloat16 or wider, within the bound.
A program may use at most 128 MiB of HBM per device.

v0:
```python
import jax
import jax.numpy as jnp
from jax import lax
from jax.sharding import PartitionSpec as P

BLOCK = 64


coherence = 128.0
loss_grad = 1.0 / 32.0
epsilon = 1e-06


def coherence_weights(raw_rows, norm_rows, norm_all, alive_rows, alive_all):
    row_total, extent = raw_rows.shape
    row_ids = jnp.arange(row_total)[:, None]
    col_ids = jnp.arange(extent)[None, :]
    norm_pair = norm_rows[:, None] * norm_all[None, :]
    cosine = raw_rows / norm_pair
    on_diagonal = row_ids == col_ids
    coupled = jnp.where(on_diagonal, 0.0, alive_rows[:, None] * alive_all[None, :] * cosine)
    spread = jnp.sum(coupled * cosine, axis=1)
    diag_term = jnp.where(on_diagonal, (spread / (norm_rows * norm_rows))[:, None], 0.0)
    return (4.0 * coherence * (coupled / norm_pair - diag_term)).astype(jnp.bfloat16)


def picked_pair(table, hit_a, hit_b):
    first_pick = jnp.sum(jnp.where(hit_a, table, 0.0), axis=1)
    second_pick = jnp.sum(jnp.where(hit_b, table, 0.0), axis=1)
    return (first_pick, second_pick)


def per_device(tokens, dec_bias, encoder, enc_bias, decoder, atom_ids, block_count):
    tok_dev, width_shard = tokens.shape
    atom_dev = encoder.shape[0]
    owner_total = lax.axis_size("atoms")
    pair_total = atom_ids.shape[1] // 2
    capacity = 3 * tok_dev * pair_total // (2 * owner_total)
    slot_total = owner_total * capacity
    contract = (((1,), (1,)), ((), ()))
    contract_rows = (((0,), (0,)), ((), ()))
    centered = (tokens.astype(jnp.float32) - dec_bias).astype(jnp.bfloat16)
    pair_ids = atom_ids.reshape(tok_dev * pair_total, 2)
    owner_of = pair_ids[:, 0] // atom_dev
    local_atom = pair_ids % atom_dev
    member = (owner_of[:, None] == jnp.arange(owner_total)[None, :]).astype(jnp.int32)
    before = jnp.cumsum(member, axis=0) - member
    slot_of = owner_of * capacity + jnp.sum(before * member, axis=1)
    source_tok = jnp.arange(tok_dev * pair_total) // pair_total
    outgoing = (
        jnp.zeros((slot_total, width_shard), jnp.bfloat16).at[slot_of].set(centered[source_tok])
    )
    slot_tags = jnp.concatenate([local_atom, source_tok[:, None]], axis=1)
    tag_out = jnp.full((slot_total, 3), -1, jnp.int32).at[slot_of].set(slot_tags)
    incoming = lax.all_to_all(outgoing, "atoms", split_axis=0, concat_axis=0, tiled=True)
    tag_in = lax.all_to_all(tag_out, "atoms", split_axis=0, concat_axis=0, tiled=True)
    columns = jnp.arange(atom_dev)[None, :]
    hit_a = tag_in[:, 0:1] == columns
    hit_b = tag_in[:, 1:2] == columns
    scores = lax.dot_general(incoming, encoder, contract, preferred_element_type=jnp.float32)
    scores = lax.psum(scores.astype(jnp.bfloat16), "width").astype(jnp.float32)
    pre_a, pre_b = picked_pair(scores, hit_a, hit_b)
    bias_a, bias_b = picked_pair(enc_bias[None, :], hit_a, hit_b)
    act_a = (pre_a + bias_a).astype(jnp.bfloat16)
    act_b = (pre_b + bias_b).astype(jnp.bfloat16)
    zero_low = jnp.zeros((), jnp.bfloat16)
    act_table = jnp.where(hit_a, act_a[:, None], zero_low) + jnp.where(
        hit_b, act_b[:, None], zero_low
    )
    decoded = jnp.dot(act_table, decoder, preferred_element_type=jnp.float32).astype(jnp.bfloat16)
    returned = lax.all_to_all(decoded, "atoms", split_axis=0, concat_axis=0, tiled=True)
    own_terms = returned[slot_of].reshape(tok_dev, pair_total, width_shard).astype(jnp.float32)
    residual = (jnp.sum(own_terms, axis=1) + dec_bias - tokens.astype(jnp.float32)).astype(
        jnp.bfloat16
    )
    token_of_slot = jnp.maximum(tag_in[:, 2], 0)
    piece = lax.all_gather(residual, "atoms", axis=0, tiled=True)
    rows = piece.shape[0]
    src_count = rows // tok_dev
    offset = jnp.arange(src_count * capacity) // capacity * tok_dev
    picked = piece[token_of_slot + offset]
    back_scores = lax.dot_general(picked, decoder, contract, preferred_element_type=jnp.float32)
    back_scores = lax.psum(back_scores.astype(jnp.bfloat16), "width").astype(jnp.float32)
    grad_a, grad_b = picked_pair(back_scores, hit_a, hit_b)
    dact_a = grad_a * loss_grad
    dact_b = grad_b * loss_grad
    dact_table = jnp.where(hit_a, dact_a[:, None], 0.0) + jnp.where(hit_b, dact_b[:, None], 0.0)
    bias_grad = jnp.sum(dact_table, axis=0)
    encoder_grad = lax.dot_general(
        dact_table.astype(jnp.bfloat16), incoming, contract_rows, preferred_element_type=jnp.float32
    ).astype(jnp.bfloat16)
    fitted = (
        lax.dot_general(act_table, picked, contract_rows, preferred_element_type=jnp.float32)
        * loss_grad
    )
    raw_gram = lax.dot_general(decoder, decoder, contract, preferred_element_type=jnp.float32)
    alive = (jnp.arange(atom_dev) < block_count[0] * BLOCK).astype(jnp.float32)
    summed = lax.psum(raw_gram, "width")
    norms = jnp.sqrt(jnp.diagonal(summed) + epsilon)
    weights = coherence_weights(summed, norms, norms, alive, alive)
    penalty = jnp.dot(weights, decoder, preferred_element_type=jnp.float32)
    decoder_grad = (fitted + penalty).astype(jnp.bfloat16)
    return (residual, encoder_grad, decoder_grad, bias_grad)


def solution(mesh):
    in_specs = (
        P("atoms", "width"),
        P("width"),
        P("atoms", "width"),
        P("atoms"),
        P("atoms", "width"),
        P("atoms", None),
        P("atoms"),
    )
    out_specs = (P("atoms", "width"), P("atoms", "width"), P("atoms", "width"), P("atoms"))
    return jax.shard_map(
        per_device, mesh=mesh, in_specs=in_specs, out_specs=out_specs, check_vma=False
    )
```

profile of v0, /device:TPU:0, one launch (start us, length us, event | category | flops | bytes accessed | tf_op | source)
XLA Modules:
  0.0 885.7 jit_solution(3246302355869958463)
XLA Ops:
  7.2 0.0 all-reduce.4.cloned.1.call-start
  7.2 0.2 fusion.18
  7.4 0.8 copy.39
  8.3 0.2 reshape.164
  8.5 0.4 fusion.58
  8.9 4.5 reduce-window.6
  13.4 0.1 slice.33
  13.5 0.1 copy.40
  13.6 0.1 copy.41
  13.7 0.1 broadcast_add_fusion
  13.9 0.2 copy.42
  14.1 0.5 add_select_fusion
  14.6 1.4 fusion.3
  16.0 7.8 gather_fusion
  23.8 20.1 %scatter_custom_fusion.1 = bf16[1536,4096]{1,0:T(8,128)(2,1)} fusion(s32[1024]{0:T(1024)S(1)} %get-tuple-element.14, bf16[1024,4096]{1,0:T(8,128)(2,1)} %gather_fusion, bf16[]{:T(256)} %constant.78.clone.1), kind=kCustom, calls=%fused_computation.8 | custom fusion | bytes 12583424 | tf_op jit(solution)/shard_map/scatter | solution.py:51
  43.9 279.5 %all_to_all.36 = bf16[16,96,4096]{2,1,0:T(8,128)(2,1)S(1)} all-to-all(bf16[16,96,4096]{2,1,0:T(8,128)(2,1)} %bitcast.46), channel_id=1, replica_groups=mesh['atoms'=16,'width'=2] {'atoms'}, dimensions={0} | all-to-all | bytes 25165824 | tf_op jit(solution)/shard_map/all_to_all | solution.py:55
  323.4 4.6 copy-done.1
  328.0 4.3 convolution_convert_fusion.3
  332.3 1.0 add_select_fusion.1
  333.3 3.9 scatter_custom_fusion
  337.2 0.3 copy.43
  337.5 12.5 %all_to_all.37 = s32[16,96,3]{1,2,0:T(4,128)S(1)} all-to-all(s32[16,96,3]{1,2,0:T(4,128)S(1)} %copy.43), channel_id=1, replica_groups=mesh['atoms'=16,'width'=2] {'atoms'}, dimensions={0} | all-to-all | bytes 36864 | tf_op jit(solution)/shard_map/all_to_all | solution.py:56
  350.0 0.1 all_to_all.26
  350.1 0.1 fusion.50
  350.2 9.4 %all-reduce.4.cloned.1.call-done = bf16[1536,128]{1,0:T(8,128)(2,1)} async-done(((bf16[1536,128]{1,0:T(8,128)(2,1)}), bf16[1536,128]{1,0:T(8,128)(2,1)}) %all-reduce.4.cloned.1.call-update) | async-done | bytes 393232 | tf_op jit(solution)/shard_map/psum | solution.py:61
  359.6 2.5 fusion.5
  362.2 7.0 convolution_convert_fusion
  369.1 5.7 all-to-all-start.2
  374.8 0.0 all-reduce.8.cloned.1.call-start
  374.9 1.1 fusion.59
  376.0 0.4 all-gather.2.cloned.1.call-start
  376.4 222.1 %all-to-all-done.2 = bf16[16,96,4096]{2,1,0:T(8,128)(2,1)} async-done(((bf16[16,96,4096]{2,1,0:T(8,128)(2,1)}), bf16[16,96,4096]{2,1,0:T(8,128)(2,1)}, u32[]{:S(2)}, u32[]{:S(2)}) %all-to-all-start.2) | async-done | bytes 12582944 | tf_op jit(solution)/shard_map/all_to_all | solution.py:71
  598.6 21.3 %gather_fusion.1 = bf16[1024,4096]{1,0:T(8,128)(2,1)} fusion(bf16[1536,4096]{1,0:T(8,128)(2,1)} %bitcast.7, s32[1024]{0:T(1024)S(1)} %broadcast_clamp_fusion), kind=kCustom, calls=%fused_computation.1 | custom fusion | bytes 16781312 | tf_op jit(solution)/shard_map/gather | solution.py:72
  619.9 9.1 %convert_reduce_fusion = f32[128,4096]{1,0:T(8,128)S(1)} fusion(bf16[1024,4096]{1,0:T(8,128)(2,1)} %gather_fusion.1), kind=kLoop, calls=%fused_computation.6 | loop fusion | flops 7864320 | bytes 10485760 | tf_op jit(solution)/shard_map/reduce_sum | solution.py:73
  628.9 2.5 fusion.4
  631.4 0.2 all-reduce.6.cloned.1.call-start
  632.3 0.0 all-reduce.8.cloned.1.call-done
  632.4 1.9 gather_fusion.3
  634.3 1.0 multiply_reduce_fusion
  635.4 170.8 %all-gather.2.cloned.1.call-done = bf16[2048,4096]{1,0:T(8,128)(2,1)} async-done(((bf16[128,4096]{1,0:T(8,128)(2,1)}), bf16[2048,4096]{1,0:T(8,128)(2,1)}) %all-gather.2.cloned.1.call-update) | async-done | bytes 16777232 | tf_op jit(solution)/shard_map/all_gather | solution.py:77
  806.2 30.0 %gather_fusion.2 = bf16[1536,4096]{1,0:T(8,128)(2,1)} fusion(bf16[2048,4096]{1,0:T(8,128)(2,1)} %all-gather.2.cloned.1.call-done, s32[2048]{0:T(1024)S(1)} %pad_clamp_fusion), kind=kCustom, calls=%fused_computation.2 | custom fusion | bytes 25171968 | tf_op jit(solution)/shard_map/gather | solution.py:81
  836.2 7.2 convolution_convert_fusion.2
  843.4 7.0 convolution_multiply_fusion
  850.5 1.5 fusion.2
  852.0 15.5 %all-reduce.6.cloned.1.call-done = bf16[1536,128]{1,0:T(8,128)(2,1)} async-done(((bf16[1536,128]{1,0:T(8,128)(2,1)}), bf16[1536,128]{1,0:T(8,128)(2,1)}) %all-reduce.6.cloned.1.call-update) | async-done | bytes 393232 | tf_op jit(solution)/shard_map/psum | solution.py:83
  867.5 2.1 fusion.7
  869.6 1.8 fusion.9
  871.4 7.6 convolution_convert_fusion.1
  (31 shorter events, 0.2 us)
Async XLA Ops:
  7.2 355.0 %copy-start = (bf16[128,4096]{1,0:T(8,128)(2,1)S(1)}, bf16[128,4096]{1,0:T(8,128)(2,1)}, u32[]{:S(2)}) copy-start(bf16[128,4096]{1,0:T(8,128)(2,1)} %param.11) | copy-start | bytes 3145732
  7.2 352.4 %all-reduce.4.cloned.1.call-start = ((), (), s32[]{:S(2)}) async-start(), calls=%async_computation.3 | async-start | bytes 786432 | tf_op jit(solution)/shard_map/psum | solution.py:61
  43.9 284.1 %copy-start.5 = (bf16[128,4096]{1,0:T(8,128)(2,1)S(1)}, bf16[128,4096]{1,0:T(8,128)(2,1)}, u32[]{:S(2)}) copy-start(bf16[128,4096]{1,0:T(8,128)(2,1)} %param.9) | copy-start | bytes 3145732
  323.4 4.6 copy-start.1
  323.4 36.2 %copy-start.4 = (f32[128]{0:T(128)S(1)}, f32[128]{0:T(128)}, u32[]{:S(2)}) copy-start(f32[128]{0:T(128)} %param.10) | copy-start | bytes 1540
  369.1 229.4 %all-to-all-start.2 = ((bf16[16,96,4096]{2,1,0:T(8,128)(2,1)}), bf16[16,96,4096]{2,1,0:T(8,128)(2,1)}, u32[]{:S(2)}, u32[]{:S(2)}) async-start(bf16[16,96,4096]{2,1,0:T(8,128)(2,1)} %bitcast.43), calls=%async_computation.2 | async-start | bytes 25165824 | tf_op jit(solution)/shard_map/all_to_all | solution.py:71
  374.8 257.6 %all-reduce.8.cloned.1.call-start = ((), (), s32[]{:S(2)}) async-start(), calls=%async_computation.6 | async-start | bytes 131072 | tf_op jit(solution)/shard_map/psum | solution.py:98
  376.0 430.2 %all-gather.2.cloned.1.call-start = ((), (), s32[]{:S(2)}) async-start(), calls=%async_computation.4 | async-start | bytes 17825792 | tf_op jit(solution)/shard_map/all_gather | solution.py:77
  598.6 30.4 %copy-start.3 = (f32[4096]{0:T(1024)S(1)}, f32[4096]{0:T(1024)}, u32[]{:S(2)}) copy-start(f32[4096]{0:T(1024)} %param.8) | copy-start | bytes 49156
  631.4 236.1 %all-reduce.6.cloned.1.call-start = ((), (), s32[]{:S(2)}) async-start(), calls=%async_computation.5 | async-start | bytes 786432 | tf_op jit(solution)/shard_map/psum | solution.py:83
  836.2 14.3 %copy-start.2 = (f32[128,128]{1,0:T(8,128)S(1)}, f32[128,128]{1,0:T(8,128)}, u32[]{:S(2)}) copy-start(f32[128,128]{1,0:T(8,128)} %all-reduce.8.cloned.1.call-done) | copy-start | bytes 196612
Sparse Core Ops, SparseCore 0:
  332.4 27.1 all-reduce.3
  378.6 21.1 all-reduce.7
  631.5 174.6 all-gather.1
  843.6 23.8 all-reduce.5
where the time goes:
time: 899 us; the launch traced here: 886 us
  waiting for transfers between devices  418 us (46%)
  blocking collectives  292 us (32%)
  local copies, waits for them, and re-layouts  87.6 us (10%)
  matrix products  35.6 us (4%)
  other arithmetic  31.1 us (3%)
  between operations  14.9 us (2%)
    all_to_all x1, blocking collectives, per_device(): lax.all_to_all(outgoing, 'atoms', split_axis=0, concat_axis=0, tiled=True)  280 us
    all_to_all x1, waiting for transfers between devices, per_device(): lax.all_to_all(decoded, 'atoms', split_axis=0, concat_axis=0, tiled=True)  222 us
    all_gather x1, waiting for transfers between devices, per_device(): piece = lax.all_gather(residual, 'atoms', axis=0, tiled=True)  171 us
    gather x1, local copies, waits for them, and re-layouts, per_device(): picked = piece[token_of_slot + offset]  30 us
    gather x1, local copies, waits for them, and re-layouts, per_device(): returned[slot_of].reshape(tok_dev, pair_total, width_shard)  21.3 us
    scatter x1, local copies, waits for them, and re-layouts, per_device(): jnp.zeros((slot_total, width_shard), jnp.bfloat16).at[slot_of]  20.1 us
  transfers between devices with their start and end apart: 5, of which 4 were waited for; matrix products, arithmetic and copies ran while one was open for 6% of the time, Pallas kernels for 0%

commit v1 on v0

--- a/solution.py
+++ b/solution.py
@@ -1,6 +1,10 @@
+import functools
+
 import jax
 import jax.numpy as jnp
 from jax import lax
+from jax.experimental import pallas as pl
+from jax.experimental.pallas import tpu as pltpu
 from jax.sharding import PartitionSpec as P
 
 BLOCK = 64
@@ -30,7 +34,7 @@
     return (first_pick, second_pick)
 
 
-def per_device(tokens, dec_bias, encoder, enc_bias, decoder, atom_ids, block_count):
+def dispatched(tokens, dec_bias, encoder, enc_bias, decoder, atom_ids, block_count):
     tok_dev, width_shard = tokens.shape
     atom_dev = encoder.shape[0]
     owner_total = lax.axis_size("atoms")
@@ -103,6 +107,304 @@
     return (residual, encoder_grad, decoder_grad, bias_grad)
 
 
+MESH = pl.DeviceIdType.MESH
+CHUNK = 32
+PLACES = 4
+
+
+def gather_kernel(n, src_ref, out_ref, send_sem, recv_sem, own_sem):
+    rows = src_ref.shape[0]
+    chunks = rows // CHUNK
+    line = n // PLACES
+    me = lax.axis_index("atoms")
+    across_width = lax.axis_index("width")
+    core = lax.rem(me, 2)
+    side = lax.rem(me // 2, 2)
+    level = me // PLACES
+    up, down = me + PLACES, me - PLACES
+    across = me + 2 - 4 * side
+    sibling = me + 1 - 2 * core
+    has_up = level < line - 1
+    has_down = level > 0
+
+    barrier = pltpu.get_barrier_semaphore()
+
+    def greet(device):
+        pl.semaphore_signal(
+            barrier, inc=1, device_id=(device, across_width), device_id_type=MESH
+        )
+
+    greet(across)
+    greet(sibling)
+
+    @pl.when(has_up)
+    def _():
+        greet(up)
+
+    @pl.when(has_down)
+    def _():
+        greet(down)
+
+    peers = 2 + has_up.astype(jnp.int32) + has_down.astype(jnp.int32)
+    pl.semaphore_wait(barrier, peers)
+
+    def piece(k):
+        return pl.ds(pl.multiple_of(k * CHUNK, CHUNK), CHUNK)
+
+    def copy(slot, k, way, device, own=False):
+        here = src_ref.at[piece(k)] if own else out_ref.at[slot, piece(k)]
+        return pltpu.make_async_remote_copy(
+            src_ref=here,
+            dst_ref=out_ref.at[slot, piece(k)],
+            send_sem=send_sem.at[slot, k, way],
+            recv_sem=recv_sem.at[slot, k],
+            device_id=(device, across_width),
+            device_id_type=MESH,
+        )
+
+    def arrived(slot, k):
+        copy(slot, k, 0, sibling).wait_recv()
+
+    def over_chunks(body):
+        def step(k, carry):
+            body(k)
+            return carry
+
+        lax.fori_loop(0, chunks, step, 0)
+
+    own_copy = pltpu.make_async_copy(src_ref, out_ref.at[me], own_sem)
+    own_copy.start()
+
+    def spread(k, act):
+        @pl.when(has_up)
+        def _():
+            act(copy(me, k, 0, up, True))
+
+        @pl.when(has_down)
+        def _():
+            act(copy(me, k, 1, down, True))
+
+        act(copy(me, k, 2, across, True))
+        act(copy(me, k, 3, sibling, True))
+
+    def pass_on(hop, k, act, wait):
+        @pl.when(level >= hop)
+        def _():
+            slot = me - PLACES * hop
+            if wait:
+                arrived(slot, k)
+
+            @pl.when(has_up)
+            def _():
+                act(copy(slot, k, 0, up))
+
+            act(copy(slot, k, 2, across))
+            act(copy(slot, k, 3, sibling))
+
+        @pl.when(level + hop < line)
+        def _():
+            slot = me + PLACES * hop
+            if wait:
+                arrived(slot, k)
+
+            @pl.when(has_down)
+            def _():
+                act(copy(slot, k, 1, down))
+
+            act(copy(slot, k, 2, across))
+            act(copy(slot, k, 3, sibling))
+
+    def hand_over(hop, k, act, wait):
+        if hop == 0:
+            if wait:
+                arrived(across, k)
+            act(copy(across, k, 3, sibling))
+            return
+
+        @pl.when(level >= hop)
+        def _():
+            slot = across - PLACES * hop
+            if wait:
+                arrived(slot, k)
+            act(copy(slot, k, 3, sibling))
+
+        @pl.when(level + hop < line)
+        def _():
+            slot = across + PLACES * hop
+            if wait:
+                arrived(slot, k)
+            act(copy(slot, k, 3, sibling))
+
+    def start(c):
+        c.start()
+
+    def sent(c):
+        c.wait_send()
+
+    over_chunks(lambda k: spread(k, start))
+    for hop in range(1, line + 1):
+
+        def turn(k, hop=hop):
+            if hop < line:
+                pass_on(hop, k, start, True)
+            hand_over(hop - 1, k, start, True)
+
+        over_chunks(turn)
+
+    def last(k):
+        for place in range(n // 2):
+            arrived(2 * place + 1 - core, k)
+
+    over_chunks(last)
+
+    def drain(k):
+        spread(k, sent)
+        for hop in range(line):
+            if hop:
+                pass_on(hop, k, sent, False)
+            hand_over(hop, k, sent, False)
+
+    over_chunks(drain)
+    own_copy.wait()
+
+
+def gathered(x, n, collective_id):
+    rows, width = x.shape
+    chunks = rows // CHUNK
+    return pl.pallas_call(
+        functools.partial(gather_kernel, n),
+        out_shape=jax.ShapeDtypeStruct((n, rows, width), x.dtype),
+        in_specs=[pl.BlockSpec(memory_space=pl.ANY)],
+        out_specs=pl.BlockSpec(memory_space=pl.ANY),
+        scratch_shapes=[
+            pltpu.SemaphoreType.DMA((n, chunks, 4)),
+            pltpu.SemaphoreType.DMA((n, chunks)),
+            pltpu.SemaphoreType.DMA,
+        ],
+        compiler_params=pltpu.CompilerParams(collective_id=collective_id, has_side_effects=True),
+        cost_estimate=pl.CostEstimate(
+            flops=0, bytes_accessed=16 * n * rows * width, transcendentals=0
+        ),
+        name=f"gather_{collective_id}",
+    )(x)
+
+
+def decode_kernel(act_ref, dec_ref, tok_ref, bias_ref, out_ref, total):
+    step = pl.program_id(0)
+    width = tok_ref.shape[1]
+    tile = min(width, 512)
+
+    @pl.when(step == 0)
+    def _():
+        total[...] = jnp.broadcast_to(bias_ref[...], total.shape)
+
+    for at in range(0, width, tile):
+        cols = pl.ds(at, tile)
+        term = jnp.dot(act_ref[0], dec_ref[0, :, cols], preferred_element_type=jnp.float32)
+        total[:, cols] += term.astype(jnp.bfloat16).astype(jnp.float32)
+
+    @pl.when(step == pl.num_programs(0) - 1)
+    def _():
+        for at in range(0, width, tile):
+            cols = pl.ds(at, tile)
+            out_ref[:, cols] = (total[:, cols] - tok_ref[:, cols].astype(jnp.float32)).astype(
+                jnp.bfloat16
+            )
+
+
+def decode(acts, rows, tokens, dec_bias):
+    n, atom_dev, width = rows.shape
+    tok_dev = tokens.shape[0]
+    return pl.pallas_call(
+        decode_kernel,
+        grid=(n,),
+        out_shape=jax.ShapeDtypeStruct(tokens.shape, jnp.bfloat16),
+        in_specs=[
+            pl.BlockSpec((1, tok_dev, atom_dev), lambda o: (o, 0, 0)),
+            pl.BlockSpec((1, atom_dev, width), lambda o: (o, 0, 0)),
+            pl.BlockSpec((tok_dev, width), lambda o: (0, 0)),
+            pl.BlockSpec((1, width), lambda o: (0, 0)),
+        ],
+        out_specs=pl.BlockSpec((tok_dev, width), lambda o: (0, 0)),
+        scratch_shapes=[pltpu.VMEM((tok_dev, width), jnp.float32)],
+        compiler_params=pltpu.CompilerParams(vmem_limit_bytes=32 * 1024 * 1024),
+        name="decode",
+    )(acts, rows, tokens, dec_bias[None, :])
+
+
+def collected(tokens, dec_bias, encoder, enc_bias, decoder, atom_ids, block_count):
+    tok_dev, width_shard = tokens.shape
+    atom_dev = encoder.shape[0]
+    owner_total = lax.axis_size("atoms")
+    pick = atom_ids.shape[1]
+    token_total = owner_total * tok_dev
+    contract = (((1,), (1,)), ((), ()))
+    contract_rows = (((0,), (0,)), ((), ()))
+    wide = jnp.float32
+    centered = (tokens.astype(wide) - dec_bias).astype(jnp.bfloat16)
+    ids_all = lax.all_gather(atom_ids, "atoms", axis=0, tiled=True)
+    raw_gram = lax.dot_general(decoder, decoder, contract, preferred_element_type=wide)
+    summed = lax.psum(raw_gram, "width")
+    centered_all = gathered(centered, owner_total, 1).reshape(token_total, width_shard)
+    scores = lax.dot_general(centered_all, encoder, contract, preferred_element_type=wide)
+    scores = lax.psum(scores.astype(jnp.bfloat16), "width").astype(wide)
+    columns = lax.axis_index("atoms") * atom_dev + jnp.arange(atom_dev)[None, :]
+    hit = functools.reduce(
+        jnp.logical_or, [ids_all[:, k : k + 1] == columns for k in range(pick)]
+    )
+    act_table = jnp.where(hit, scores + enc_bias[None, :], 0.0).astype(jnp.bfloat16)
+    acts = lax.all_to_all(
+        act_table.reshape(owner_total, tok_dev, atom_dev), "atoms", split_axis=0, concat_axis=0, tiled=True
+    )
+    decoder_all = gathered(decoder, owner_total, 2)
+    residual = decode(acts, decoder_all, tokens, dec_bias)
+    back = lax.dot_general(
+        residual,
+        decoder_all.reshape(owner_total * atom_dev, width_shard),
+        contract,
+        preferred_element_type=wide,
+    )
+    slots = jnp.arange(owner_total * atom_dev)[None, :]
+    picked = jnp.stack(
+        [jnp.sum(jnp.where(atom_ids[:, k : k + 1] == slots, back, 0.0), axis=1) for k in range(pick)],
+        axis=1,
+    )
+    dact = lax.psum(picked, "width") * loss_grad
+    dact_all = lax.all_gather(dact, "atoms", axis=0, tiled=True)
+    residual_all = gathered(residual, owner_total, 3).reshape(token_total, width_shard)
+    dact_table = functools.reduce(
+        jnp.add,
+        [
+            jnp.where(ids_all[:, k : k + 1] == columns, dact_all[:, k : k + 1], 0.0)
+            for k in range(pick)
+        ],
+    )
+    bias_grad = jnp.sum(dact_table, axis=0)
+    encoder_grad = lax.dot_general(
+        dact_table.astype(jnp.bfloat16), centered_all, contract_rows, preferred_element_type=wide
+    ).astype(jnp.bfloat16)
+    alive = (jnp.arange(atom_dev) < block_count[0] * BLOCK).astype(wide)
+    norms = jnp.sqrt(jnp.diagonal(summed) + epsilon)
+    weights = coherence_weights(summed, norms, norms, alive, alive)
+    penalty = jnp.dot(weights, decoder, preferred_element_type=wide)
+    fitted = (
+        lax.dot_general(act_table, residual_all, contract_rows, preferred_element_type=wide)
+        * loss_grad
+    )
+    decoder_grad = (fitted + penalty).astype(jnp.bfloat16)
+    return (residual, encoder_grad, decoder_grad, bias_grad)
+
+
+GATHER_BYTES = 32 * 1024 * 1024
+
+
+def per_device(tokens, *others):
+    owners = lax.axis_size("atoms")
+    room = owners * tokens.size * tokens.dtype.itemsize <= GATHER_BYTES
+    even = owners % PLACES == 0 and tokens.shape[0] % CHUNK == 0
+    return (collected if room and even else dispatched)(tokens, *others)
+
+
 def solution(mesh):
     in_specs = (
         P("atoms", "width"),

time: 899 us -> 454 us (0.51); the launches traced: 886 us -> 453 us
  waiting for transfers between devices: 418 us -> 11.4 us
  Pallas kernels: 0 us -> 304 us
  blocking collectives: 292 us -> 45.8 us
  local copies, waits for them, and re-layouts: 87.6 us -> 8 us
  other arithmetic: 31.1 us -> 20.6 us
  matrix products: 35.6 us -> 45.2 us
    pallas_call x0 -> x4, Pallas kernels: none -> 304 us  [the longest x3 295 us: gathered(): pl.pallas_call(functools.partial(gather_kernel, n), out_shape=jax.ShapeDt...]
    all_to_all x2 -> x0, blocking collectives: 292 us -> none  [the longest x1 280 us: per_device(): lax.all_to_all(outgoing, 'atoms', split_axis=0, concat_axis=0, tiled=True)]
    all_to_all x1, waiting for transfers between devices: 222 us -> 11.4 us  [collected(): lax.all_to_all(act_table.reshape(owner_total, tok_dev, atom_dev), 'atoms'...]
    all_gather x1 -> x0, waiting for transfers between devices: 171 us -> none  [per_device(): piece = lax.all_gather(residual, 'atoms', axis=0, tiled=True)]
    gather x4 -> x1, local copies, waits for them, and re-layouts: 61 us -> 1.94 us  [collected(): norms = jnp.sqrt(jnp.diagonal(summed) + epsilon)]
    all_gather x0 -> x2, blocking collectives: none -> 40.8 us  [the longest x1 20.8 us: collected(): ids_all = lax.all_gather(atom_ids, 'atoms', axis=0, tiled=True)]
    psum x3 -> x2, waiting for transfers between devices: 25 us -> 0.04 us  [the longest x1 0.02 us: collected(): summed = lax.psum(raw_gram, 'width')]
    scatter x1 -> x0, local copies, waits for them, and re-layouts: 20.1 us -> none  [per_device(): jnp.zeros((slot_total, width_shard), jnp.bfloat16).at[slot_of]]
  transfers between devices with their start and end apart: 5 -> 3, of which waited for: 4 -> 1; matrix products, arithmetic and copies ran while one was open for 6% -> 3% of each run, Pallas kernels for 0% -> 22%
where the time goes in v1:
time: 454 us; the launch traced here: 453 us
  Pallas kernels  304 us (67%)
  blocking collectives  45.8 us (10%)
  matrix products  45.2 us (10%)
  other arithmetic  20.6 us (5%)
  between operations  14.9 us (3%)
  waiting for transfers between devices  11.4 us (3%)
  local copies, waits for them, and re-layouts  8 us (2%)
    pallas_call x3, Pallas kernels, gathered(): pl.pallas_call(functools.partial(gather_kernel, n), out_shape=jax.ShapeDt...  295 us
    all_gather x1, blocking collectives, collected(): ids_all = lax.all_gather(atom_ids, 'atoms', axis=0, tiled=True)  20.8 us
    all_gather x1, blocking collectives, collected(): dact_all = lax.all_gather(dact, 'atoms', axis=0, tiled=True)  20 us
    dot_general x1, matrix products, collected(): lax.dot_general(dact_table.astype(jnp.bfloat16), centered_all, contract_r...  17.7 us
    dot_general x1, matrix products, collected(): lax.dot_general(residual, decoder_all.reshape(owner_total * atom_dev, wid...  12.5 us
    all_to_all x1, waiting for transfers between devices, collected(): lax.all_to_all(act_table.reshape(owner_total, tok_dev, atom_dev), 'atoms'...  11.4 us
    reduce_sum x1, other arithmetic, collected(): bias_grad = jnp.sum(dact_table, axis=0)  9.84 us
  transfers between devices with their start and end apart: 3, of which 1 were waited for; matrix products, arithmetic and copies ran while one was open for 3% of the time, Pallas kernels for 22%

profile of v1, /device:TPU:0, one launch (start us, length us, event | category | flops | bytes accessed | tf_op | source)
XLA Modules:
  0.0 453.3 jit_solution(1851055295628545149)
XLA Ops:
  7.2 0.0 copy-start
  7.2 0.0 all-reduce.3.cloned.1.call-start
  7.2 2.5 subtract_convert_fusion.src_ref
  9.7 99.5 %gather_1.1 = bf16[16,128,4096]{2,1,0:T(8,128)(2,1)} custom-call(bf16[128,4096]{1,0:T(8,128)(2,1)} %subtract_convert_fusion.src_ref), custom_call_target="tpu_custom_call" | custom-call | bytes 134217728 | tf_op jit(solution)/shard_map/gather_1/pallas_call | solution.py:274
  109.2 0.0 copy-start.5
  109.3 0.0 copy-done
  109.3 0.0 copy-start.9
  109.3 9.1 %convolution_convert_fusion.1 = bf16[2048,128]{1,0:T(8,128)(2,1)} fusion(bf16[2048,4096]{1,0:T(8,128)(2,1)} %bitcast.102, bf16[128,4096]{1,0:T(8,128)(2,1)S(1)} %copy-done), kind=kOutput, calls=%fused_computation.5 | convolution fusion | flops 2147745792 | bytes 18350080 | tf_op jit(solution)/shard_map/dot_general | solution.py:349
  118.3 0.0 copy-start.10
  118.3 0.0 copy-start.2
  118.3 0.0 copy-start.3
  118.3 0.0 all-reduce.3.cloned.1.call-update
  118.4 0.0 all-reduce.5.cloned.1.call-start
  118.4 0.0 copy-done.5
  118.4 1.1 fusion.34
  119.5 0.0 all-reduce.5.cloned.1.call-update
  119.5 98.0 %gather_2.1.dec_ref = bf16[16,128,4096]{2,1,0:T(8,128)(2,1)} custom-call(bf16[128,4096]{1,0:T(8,128)(2,1)} %src_ref.1), custom_call_target="tpu_custom_call" | custom-call | bytes 134217728 | tf_op jit(solution)/shard_map/gather_2/pallas_call | solution.py:274
  217.6 0.0 copy-done.9
  217.6 20.8 %all_gather.6 = s32[2048,16]{0,1:T(8,128)S(1)} all-gather(s32[128,16]{0,1:T(8,128)S(1)} %copy-done.9), channel_id=1, replica_groups=mesh['atoms'=16,'width'=2] {'atoms'}, dimensions={0}, use_global_device_ids=true | all-gather | bytes 139264 | tf_op jit(solution)/shard_map/all_gather | solution.py:345
  238.4 0.1 fusion.33
  239.2 0.0 all-reduce.3.cloned.1.call-done
  239.2 0.0 copy-done.10
  239.2 7.2 %select_convert_fusion = bf16[2048,128]{1,0:T(8,128)(2,1)} fusion(bf16[2048,128]{1,0:T(8,128)(2,1)} %all-reduce.3.cloned.1.call-done, f32[128]{0:T(128)S(1)} %copy-done.10, s32[128]{0:T(128)S(1)} %iota_add_fusion, s32[2048]{0:T(1024)S(1)} %bitcast.107, s32[2048]{0:T(1024)S(1)} %bitcast.110, s32[2048]{0:T(1024)S(1)} %bitcast.113, s32[2048]{0:T(1024)S(1)} %bitcast.116, ...), kind=kLoop, calls=%fused_computation.85 | loop fusion | flops 9175040 | bytes 1180672 | tf_op jit(solution)/shard_map/convert_element_type | solution.py:355
  246.4 3.6 all-to-all-start
  250.0 0.0 all-reduce.5.cloned.1.call-done
  250.1 1.9 gather_fusion
  252.0 1.0 multiply_reduce_fusion
  253.0 11.4 %all-to-all-done.act_ref = bf16[16,128,128]{2,1,0:T(8,128)(2,1)S(1)} async-done(((bf16[16,128,128]{2,1,0:T(8,128)(2,1)}), bf16[16,128,128]{2,1,0:T(8,128)(2,1)S(1)}, u32[]{:S(2)}, u32[]{:S(2)}) %all-to-all-start) | async-done | bytes 524320 | tf_op jit(solution)/shard_map/all_to_all | solution.py:356
  264.4 0.0 copy-done.2
  264.4 0.0 copy-done.3
  264.4 0.0 copy-start.1
  264.4 5.8 %copy-done.1 = bf16[16,128,4096]{2,1,0:T(8,128)(2,1)S(1)} copy-done((bf16[16,128,4096]{2,1,0:T(8,128)(2,1)S(1)}, bf16[16,128,4096]{2,1,0:T(8,128)(2,1)}, u32[]{:S(2)}) %copy-start.1) | copy-done | bytes 16777240
  270.2 8.3 %decode.1.src_ref = bf16[128,4096]{1,0:T(8,128)(2,1)} custom-call(bf16[16,128,128]{2,1,0:T(8,128)(2,1)S(1)} %all-to-all-done.act_ref, bf16[16,128,4096]{2,1,0:T(8,128)(2,1)S(1)} %copy-done.1, bf16[128,4096]{1,0:T(8,128)(2,1)S(1)} %copy-done.2, f32[1,4096]{1,0:T(1,128)S(1)} %bitcast.100), custom_call_target="tpu_custom_call" | custom-call | tf_op jit(solution)/shard_map/decode/pallas_call | solution.py:318
  278.5 97.8 %gather_3.1 = bf16[16,128,4096]{2,1,0:T(8,128)(2,1)} custom-call(bf16[128,4096]{1,0:T(8,128)(2,1)} %decode.1.src_ref), custom_call_target="tpu_custom_call" | custom-call | bytes 134217728 | tf_op jit(solution)/shard_map/gather_3/pallas_call | solution.py:274
  376.3 0.0 copy-done.8
  376.4 12.5 %select_reduce_fusion = (f32[128]{0:T(128)S(1)}, f32[128]{0:T(128)S(1)}, f32[128]{0:T(128)S(1)}, f32[128]{0:T(128)S(1)}, f32[128]{0:T(128)S(1)}, /*index=5*/f32[...) fusion(s32[128]{0:T(128)S(1)} %get-tuple-element.66, ...), kind=kOutput, calls=%fused_computation.53 | convolution fusion | flops 2160066560 | bytes 17842176 | tf_op jit(solution)/shard_map/dot_general | solution.py:361
  388.8 0.1 stack.67
  388.9 5.0 %psum.22 = f32[128,16]{0,1:T(8,128)S(1)} all-reduce(f32[128,16]{0,1:T(8,128)S(1)} %stack.67), channel_id=1, replica_groups=mesh['atoms'=16,'width'=2] {'width'}, use_global_device_ids=true, to_apply=%region_17.18 | all-reduce | flops 2048 | bytes 16384 | tf_op jit(solution)/shard_map/psum | solution.py:372
  393.9 20.0 %all_gather.7 = f32[2048,16]{0,1:T(8,128)S(1)} all-gather(f32[128,16]{0,1:T(8,128)S(1)} %broadcast_multiply_fusion), channel_id=1, replica_groups=mesh['atoms'=16,'width'=2] {'atoms'}, dimensions={0}, use_global_device_ids=true | all-gather | bytes 139264 | tf_op jit(solution)/shard_map/all_gather | solution.py:373
  413.9 0.1 fusion.32
  414.0 0.0 copy-start.4
  414.0 17.7 %convolution_convert_fusion = bf16[128,4096]{1,0:T(8,128)(2,1)} fusion(bf16[2048,4096]{1,0:T(8,128)(2,1)} %bitcast.103, f32[2048]{0:T(1024)S(1)} %bitcast.154, f32[2048]{0:T(1024)S(1)} %bitcast.156, f32[2048]{0:T(1024)S(1)} %bitcast.158, f32[2048]{0:T(1024)S(1)} %bitcast.160, f32[2048]{0:T(1024)S(1)} %bitcast.162, f32[2048]{0:T(1024)S(1)} %bitcast.164, ...), kind=kOutput, calls=%fused_computation.3 | convolution fusion | flops 2160590848 | bytes 18088448 | tf_op jit(solution)/shard_map/dot_general | solution.py:383
  431.7 9.8 %fusion.30 = f32[128]{0:T(128)} fusion(f32[2048]{0:T(1024)S(1)} %bitcast.155, s32[2048]{0:T(1024)S(1)} %bitcast.109, f32[2048]{0:T(1024)S(1)} %bitcast.157, s32[2048]{0:T(1024)S(1)} %bitcast.112, f32[2048]{0:T(1024)S(1)} %bitcast.159, s32[2048]{0:T(1024)S(1)} %bitcast.115, f32[2048]{0:T(1024)S(1)} %bitcast.161, s32[2048]{0:T(1024)S(1)} %bitcast.118, ...), kind=kLoop, calls=%fused_computation.126 | loop fusion | flops 12582784 | bytes 263168 | tf_op jit(solution)/shard_map/reduce_sum | solution.py:382
  441.6 0.0 copy-done.4
  441.6 3.4 convolution_multiply_fusion
  445.0 0.0 copy-done.6
  445.0 0.0 copy-done.7
  445.0 1.5 fusion
  (10 shorter events, 0.1 us)
Async XLA Ops:
  7.2 102.1 %copy-start = (bf16[128,4096]{1,0:T(8,128)(2,1)S(1)}, bf16[128,4096]{1,0:T(8,128)(2,1)}, u32[]{:S(2)}) copy-start(bf16[128,4096]{1,0:T(8,128)(2,1)} %param.9) | copy-start | bytes 3145732
  7.2 232.0 %all-reduce.3.cloned.1.call-start = ((), (), s32[]{:S(2)}) async-start(), calls=%async_computation.1 | async-start | bytes 1048576 | tf_op jit(solution)/shard_map/psum | solution.py:350
  109.2 9.2 %copy-start.5 = (bf16[128,4096]{1,0:T(8,128)(2,1)S(1)}, bf16[128,4096]{1,0:T(8,128)(2,1)}, u32[]{:S(2)}) copy-start(bf16[128,4096]{1,0:T(8,128)(2,1)} %src_ref.1) | copy-start | bytes 3145732
  109.3 108.3 %copy-start.9 = (s32[128,16]{0,1:T(8,128)S(1)}, s32[128,16]{0,1:T(8,128)}, u32[]{:S(2)}) copy-start(s32[128,16]{0,1:T(8,128)} %param.12) | copy-start | bytes 24580
  118.3 120.9 %copy-start.10 = (f32[128]{0:T(128)S(1)}, f32[128]{0:T(128)}, u32[]{:S(2)}) copy-start(f32[128]{0:T(128)} %param.10) | copy-start | bytes 1540
  118.3 146.1 %copy-start.2 = (bf16[128,4096]{1,0:T(8,128)(2,1)S(1)}, bf16[128,4096]{1,0:T(8,128)(2,1)}, u32[]{:S(2)}) copy-start(bf16[128,4096]{1,0:T(8,128)(2,1)} %tok_ref.1) | copy-start | bytes 3145732
  118.3 146.1 %copy-start.3 = (f32[4096]{0:T(1024)S(1)}, f32[4096]{0:T(1024)}, u32[]{:S(2)}) copy-start(f32[4096]{0:T(1024)} %param.8) | copy-start | bytes 49156
  118.4 131.7 %all-reduce.5.cloned.1.call-start = ((), (), s32[]{:S(2)}) async-start(), calls=%async_computation.2 | async-start | bytes 131072 | tf_op jit(solution)/shard_map/psum | solution.py:347
  246.4 18.0 %all-to-all-start = ((bf16[16,128,128]{2,1,0:T(8,128)(2,1)}), bf16[16,128,128]{2,1,0:T(8,128)(2,1)S(1)}, u32[]{:S(2)}, u32[]{:S(2)}) async-start(bf16[16,128,128]{2,1,0:T(8,128)(2,1)} %bitcast.17), calls=%async_computation | async-start | bytes 1048576 | tf_op jit(solution)/shard_map/all_to_all | solution.py:356
  264.4 5.8 %copy-start.1 = (bf16[16,128,4096]{2,1,0:T(8,128)(2,1)S(1)}, bf16[16,128,4096]{2,1,0:T(8,128)(2,1)}, u32[]{:S(2)}) copy-start(bf16[16,128,4096]{2,1,0:T(8,128)(2,1)} %gather_2.1.dec_ref) | copy-start | bytes 50331652
  278.5 97.8 %copy-start.8 = (bf16[128,4096]{1,0:T(8,128)(2,1)S(1)}, bf16[128,4096]{1,0:T(8,128)(2,1)}, u32[]{:S(2)}) copy-start(bf16[128,4096]{1,0:T(8,128)(2,1)} %decode.1.src_ref) | copy-start | bytes 3145732
  414.0 27.6 %copy-start.4 = (bf16[16,128,4096]{2,1,0:T(8,128)(2,1)S(1)}, bf16[16,128,4096]{2,1,0:T(8,128)(2,1)}, u32[]{:S(2)}) copy-start(bf16[16,128,4096]{2,1,0:T(8,128)(2,1)} %gather_3.1) | copy-start | bytes 50331652
  431.7 13.3 %copy-start.6 = (bf16[128,4096]{1,0:T(8,128)(2,1)S(1)}, bf16[128,4096]{1,0:T(8,128)(2,1)}, u32[]{:S(2)}) copy-start(bf16[128,4096]{1,0:T(8,128)(2,1)} %src_ref.1) | copy-start | bytes 3145732
  431.7 13.3 %copy-start.7 = (f32[128,128]{1,0:T(8,128)S(1)}, f32[128,128]{1,0:T(8,128)}, u32[]{:S(2)}) copy-start(f32[128,128]{1,0:T(8,128)} %all-reduce.5.cloned.1.call-done) | copy-start | bytes 196612
Sparse Core Ops, SparseCore 0:
  118.5 29.0 all-reduce.2
  150.5 20.7 all-reduce.4

commit v2 on v1

--- a/solution.py
+++ b/solution.py
@@ -109,12 +109,18 @@
 
 MESH = pl.DeviceIdType.MESH
 CHUNK = 32
+HEAD = 16
 PLACES = 4
 
 
-def gather_kernel(n, src_ref, out_ref, send_sem, recv_sem, own_sem):
+def gather_kernel(n, tagged, *refs):
+    if tagged:
+        src_ref, tag_ref, out_ref, tags_ref, send_sem, recv_sem, own_sem = refs
+    else:
+        src_ref, out_ref, send_sem, recv_sem, own_sem = refs
     rows = src_ref.shape[0]
-    chunks = rows // CHUNK
+    chunks = (rows - HEAD) // CHUNK
+    rest = rows - HEAD - chunks * CHUNK
     line = n // PLACES
     me = lax.axis_index("atoms")
     across_width = lax.axis_index("width")
@@ -148,16 +154,28 @@
     peers = 2 + has_up.astype(jnp.int32) + has_down.astype(jnp.int32)
     pl.semaphore_wait(barrier, peers)
 
+    TAG, FIRST, LAST = "tag", "first", "last"
+
     def piece(k):
-        return pl.ds(pl.multiple_of(k * CHUNK, CHUNK), CHUNK)
+        if isinstance(k, str):
+            return pl.ds(0, HEAD) if k == FIRST else pl.ds(rows - rest, rest)
+        return pl.ds(pl.multiple_of(HEAD + k * CHUNK, HEAD), CHUNK)
+
+    def place(k):
+        return {TAG: chunks + 2, FIRST: chunks, LAST: chunks + 1}[k] if isinstance(k, str) else k
 
     def copy(slot, k, way, device, own=False):
-        here = src_ref.at[piece(k)] if own else out_ref.at[slot, piece(k)]
+        if k == TAG if isinstance(k, str) else False:
+            here = tag_ref if own else tags_ref.at[slot]
+            there = tags_ref.at[slot]
+        else:
+            here = src_ref.at[piece(k)] if own else out_ref.at[slot, piece(k)]
+            there = out_ref.at[slot, piece(k)]
         return pltpu.make_async_remote_copy(
             src_ref=here,
-            dst_ref=out_ref.at[slot, piece(k)],
-            send_sem=send_sem.at[slot, k, way],
-            recv_sem=recv_sem.at[slot, k],
+            dst_ref=there,
+            send_sem=send_sem.at[slot, place(k), way],
+            recv_sem=recv_sem.at[slot, place(k)],
             device_id=(device, across_width),
             device_id_type=MESH,
         )
@@ -166,55 +184,76 @@
         copy(slot, k, 0, sibling).wait_recv()
 
     def over_chunks(body):
+        if tagged:
+            body(TAG)
+        body(FIRST)
+
         def step(k, carry):
             body(k)
             return carry
 
         lax.fori_loop(0, chunks, step, 0)
-
-    own_copy = pltpu.make_async_copy(src_ref, out_ref.at[me], own_sem)
-    own_copy.start()
-
-    def spread(k, act):
+        if rest:
+            body(LAST)
+
+    own_copies = [pltpu.make_async_copy(src_ref, out_ref.at[me], own_sem.at[0])]
+    if tagged:
+        own_copies.append(pltpu.make_async_copy(tag_ref, tags_ref.at[me], own_sem.at[1]))
+    for c in own_copies:
+        c.start()
+
+    def early(k):
+        return isinstance(k, str) and k == FIRST
+
+    def spread(slot, k, act, own):
         @pl.when(has_up)
         def _():
-            act(copy(me, k, 0, up, True))
+            act(copy(slot, k, 0, up, own))
 
         @pl.when(has_down)
         def _():
-            act(copy(me, k, 1, down, True))
-
-        act(copy(me, k, 2, across, True))
-        act(copy(me, k, 3, sibling, True))
+            act(copy(slot, k, 1, down, own))
+
+        if own:
+            act(copy(slot, k, 2, across, own))
+        act(copy(slot, k, 3, sibling, own))
 
     def pass_on(hop, k, act, wait):
+        columns = (me, across) if early(k) else (me,)
+
         @pl.when(level >= hop)
         def _():
-            slot = me - PLACES * hop
-            if wait:
-                arrived(slot, k)
-
-            @pl.when(has_up)
-            def _():
-                act(copy(slot, k, 0, up))
-
-            act(copy(slot, k, 2, across))
-            act(copy(slot, k, 3, sibling))
+            for column in columns:
+                slot = column - PLACES * hop
+                if wait:
+                    arrived(slot, k)
+
+                @pl.when(has_up)
+                def _():
+                    act(copy(slot, k, 0, up))
+
+                if not early(k):
+                    act(copy(slot, k, 2, across))
+                act(copy(slot, k, 3, sibling))
 
         @pl.when(level + hop < line)
         def _():
-            slot = me + PLACES * hop
-            if wait:
-                arrived(slot, k)
-
-            @pl.when(has_down)
-            def _():
-                act(copy(slot, k, 1, down))
-
-            act(copy(slot, k, 2, across))
-            act(copy(slot, k, 3, sibling))
+            for column in columns:
+                slot = column + PLACES * hop
+                if wait:
+                    arrived(slot, k)
+
+                @pl.when(has_down)
+                def _():
+                    act(copy(slot, k, 1, down))
+
+                if not early(k):
+                    act(copy(slot, k, 2, across))
+                act(copy(slot, k, 3, sibling))
 
     def hand_over(hop, k, act, wait):
+        if early(k):
+            return
         if hop == 0:
             if wait:
                 arrived(across, k)
@@ -241,7 +280,9 @@
     def sent(c):
         c.wait_send()
 
-    over_chunks(lambda k: spread(k, start))
+    over_chunks(lambda k: spread(me, k, start, True))
+    arrived(across, FIRST)
+    spread(across, FIRST, start, False)
     for hop in range(1, line + 1):
 
         def turn(k, hop=hop):
@@ -252,41 +293,47 @@
         over_chunks(turn)
 
     def last(k):
-        for place in range(n // 2):
-            arrived(2 * place + 1 - core, k)
+        for spot in range(n // 2):
+            arrived(2 * spot + 1 - core, k)
 
     over_chunks(last)
 
     def drain(k):
-        spread(k, sent)
+        spread(me, k, sent, True)
+        if early(k):
+            spread(across, k, sent, False)
         for hop in range(line):
             if hop:
                 pass_on(hop, k, sent, False)
             hand_over(hop, k, sent, False)
 
     over_chunks(drain)
-    own_copy.wait()
-
-
-def gathered(x, n, collective_id):
+    for c in own_copies:
+        c.wait()
+
+
+def gathered(x, n, collective_id, tag=None):
     rows, width = x.shape
-    chunks = rows // CHUNK
-    return pl.pallas_call(
-        functools.partial(gather_kernel, n),
-        out_shape=jax.ShapeDtypeStruct((n, rows, width), x.dtype),
-        in_specs=[pl.BlockSpec(memory_space=pl.ANY)],
-        out_specs=pl.BlockSpec(memory_space=pl.ANY),
+    chunks = (rows - HEAD) // CHUNK + 3
+    arrays = [x] if tag is None else [x, tag]
+    anywhere = pl.BlockSpec(memory_space=pl.ANY)
+    out = pl.pallas_call(
+        functools.partial(gather_kernel, n, tag is not None),
+        out_shape=[jax.ShapeDtypeStruct((n, *a.shape), a.dtype) for a in arrays],
+        in_specs=[anywhere] * len(arrays),
+        out_specs=[anywhere] * len(arrays),
         scratch_shapes=[
             pltpu.SemaphoreType.DMA((n, chunks, 4)),
             pltpu.SemaphoreType.DMA((n, chunks)),
-            pltpu.SemaphoreType.DMA,
+            pltpu.SemaphoreType.DMA((2,)),
         ],
         compiler_params=pltpu.CompilerParams(collective_id=collective_id, has_side_effects=True),
         cost_estimate=pl.CostEstimate(
             flops=0, bytes_accessed=16 * n * rows * width, transcendentals=0
         ),
         name=f"gather_{collective_id}",
-    )(x)
+    )(*arrays)
+    return out[0] if tag is None else out
 
 
 def decode_kernel(act_ref, dec_ref, tok_ref, bias_ref, out_ref, total):
@@ -339,24 +386,48 @@
     pick = atom_ids.shape[1]
     token_total = owner_total * tok_dev
     contract = (((1,), (1,)), ((), ()))
-    contract_rows = (((0,), (0,)), ((), ()))
     wide = jnp.float32
     centered = (tokens.astype(wide) - dec_bias).astype(jnp.bfloat16)
-    ids_all = lax.all_gather(atom_ids, "atoms", axis=0, tiled=True)
     raw_gram = lax.dot_general(decoder, decoder, contract, preferred_element_type=wide)
     summed = lax.psum(raw_gram, "width")
-    centered_all = gathered(centered, owner_total, 1).reshape(token_total, width_shard)
-    scores = lax.dot_general(centered_all, encoder, contract, preferred_element_type=wide)
-    scores = lax.psum(scores.astype(jnp.bfloat16), "width").astype(wide)
-    columns = lax.axis_index("atoms") * atom_dev + jnp.arange(atom_dev)[None, :]
-    hit = functools.reduce(
-        jnp.logical_or, [ids_all[:, k : k + 1] == columns for k in range(pick)]
-    )
-    act_table = jnp.where(hit, scores + enc_bias[None, :], 0.0).astype(jnp.bfloat16)
-    acts = lax.all_to_all(
-        act_table.reshape(owner_total, tok_dev, atom_dev), "atoms", split_axis=0, concat_axis=0, tiled=True
-    )
-    decoder_all = gathered(decoder, owner_total, 2)
+    centered_all, ids_all = gathered(centered, owner_total, 1, atom_ids.T)
+    centered_all = centered_all.reshape(token_total, width_shard)
+    scores = lax.dot_general(encoder, centered_all, contract, preferred_element_type=wide)
+    me = lax.axis_index("atoms")
+    first_ids, second_ids = ids_all[:, 0::2, :], ids_all[:, 1::2, :]
+    owned = first_ids // atom_dev == me
+    base = me * atom_dev
+
+    def owned_row(values, blank):
+        kept = jnp.where(owned, values, blank)
+        kept = jnp.max(kept, axis=1) if blank else jnp.sum(kept, axis=1)
+        return lax.optimization_barrier(kept.reshape(1, token_total))
+
+    atoms = jnp.arange(atom_dev)
+    hit_a = owned_row(first_ids - base, -1) == atoms[:, None]
+    hit_b = owned_row(second_ids - base, -1) == atoms[:, None]
+
+    def picked_row(table, hit):
+        return jnp.sum(jnp.where(hit, table, 0.0), axis=0)
+
+    pre = lax.psum(jnp.stack([picked_row(scores, hit_a), picked_row(scores, hit_b)]), "width")
+    biases = jnp.stack(
+        [picked_row(enc_bias[:, None], hit_a), picked_row(enc_bias[:, None], hit_b)]
+    )
+    act_pair = (pre + biases).astype(jnp.bfloat16).astype(wide)
+    decoder_all, acts_all = gathered(
+        decoder, owner_total, 2, act_pair.reshape(2 * owner_total, tok_dev)
+    )
+    act_a = lax.dynamic_index_in_dim(acts_all, me, 1, keepdims=False)
+    act_b = lax.dynamic_index_in_dim(acts_all, owner_total + me, 1, keepdims=False)
+    first, second = atom_ids[:, 0::2].T, atom_ids[:, 1::2].T
+    of_owner = first[None] // atom_dev == jnp.arange(owner_total)[:, None, None]
+    local_a = jnp.max(jnp.where(of_owner, first[None] % atom_dev, -1), axis=1)
+    local_b = jnp.max(jnp.where(of_owner, second[None] % atom_dev, -1), axis=1)
+    acts = (
+        jnp.where(local_a[:, :, None] == atoms, act_a[:, :, None], 0.0)
+        + jnp.where(local_b[:, :, None] == atoms, act_b[:, :, None], 0.0)
+    ).astype(jnp.bfloat16)
     residual = decode(acts, decoder_all, tokens, dec_bias)
     back = lax.dot_general(
         residual,
@@ -366,31 +437,26 @@
     )
     slots = jnp.arange(owner_total * atom_dev)[None, :]
     picked = jnp.stack(
-        [jnp.sum(jnp.where(atom_ids[:, k : k + 1] == slots, back, 0.0), axis=1) for k in range(pick)],
-        axis=1,
+        [jnp.sum(jnp.where(atom_ids[:, k : k + 1] == slots, back, 0.0), axis=1) for k in range(pick)]
     )
     dact = lax.psum(picked, "width") * loss_grad
-    dact_all = lax.all_gather(dact, "atoms", axis=0, tiled=True)
-    residual_all = gathered(residual, owner_total, 3).reshape(token_total, width_shard)
-    dact_table = functools.reduce(
-        jnp.add,
-        [
-            jnp.where(ids_all[:, k : k + 1] == columns, dact_all[:, k : k + 1], 0.0)
-            for k in range(pick)
-        ],
-    )
-    bias_grad = jnp.sum(dact_table, axis=0)
-    encoder_grad = lax.dot_general(
-        dact_table.astype(jnp.bfloat16), centered_all, contract_rows, preferred_element_type=wide
-    ).astype(jnp.bfloat16)
+    residual_all, dact_all = gathered(residual, owner_total, 3, dact)
+    residual_all = residual_all.reshape(token_total, width_shard)
+    dact_a = owned_row(dact_all[:, 0::2, :], 0.0)
+    dact_b = owned_row(dact_all[:, 1::2, :], 0.0)
+    dact_table = jnp.where(hit_a, dact_a, 0.0) + jnp.where(hit_b, dact_b, 0.0)
+    bias_grad = jnp.sum(dact_table, axis=1)
+    dact_low = lax.optimization_barrier(dact_table.astype(jnp.bfloat16))
+    encoder_grad = jnp.dot(dact_low, centered_all, preferred_element_type=wide).astype(
+        jnp.bfloat16
+    )
+    act_table = jnp.where(hit_a, act_pair[0:1], 0.0) + jnp.where(hit_b, act_pair[1:2], 0.0)
+    act_table = lax.optimization_barrier(act_table.astype(jnp.bfloat16))
     alive = (jnp.arange(atom_dev) < block_count[0] * BLOCK).astype(wide)
     norms = jnp.sqrt(jnp.diagonal(summed) + epsilon)
     weights = coherence_weights(summed, norms, norms, alive, alive)
     penalty = jnp.dot(weights, decoder, preferred_element_type=wide)
-    fitted = (
-        lax.dot_general(act_table, residual_all, contract_rows, preferred_element_type=wide)
-        * loss_grad
-    )
+    fitted = jnp.dot(act_table, residual_all, preferred_element_type=wide) * loss_grad
     decoder_grad = (fitted + penalty).astype(jnp.bfloat16)
     return (residual, encoder_grad, decoder_grad, bias_grad)
 
@@ -401,7 +467,7 @@
 def per_device(tokens, *others):
     owners = lax.axis_size("atoms")
     room = owners * tokens.size * tokens.dtype.itemsize <= GATHER_BYTES
-    even = owners % PLACES == 0 and tokens.shape[0] % CHUNK == 0
+    even = owners % PLACES == 0 and tokens.shape[0] % HEAD == 0
     return (collected if room and even else dispatched)(tokens, *others)
 
 

time: 454 us -> 391 us (0.86)
  blocking collectives: 45.8 us -> 13.2 us
  other arithmetic: 20.6 us -> 6.73 us
  waiting for transfers between devices: 11.4 us -> 0.02 us
  local copies, waits for them, and re-layouts: 8 us -> 15.4 us
  Pallas kernels: 304 us -> 297 us
    all_gather x2 -> x0, blocking collectives: 40.8 us -> none  [the longest x1 20.8 us: collected(): ids_all = lax.all_gather(atom_ids, 'atoms', axis=0, tiled=True)]
    all_to_all x1 -> x0, waiting for transfers between devices: 11.4 us -> none  [collected(): lax.all_to_all(act_table.reshape(owner_total, tok_dev, atom_dev), 'atoms'...]
    reduce_sum x1 -> x2, other arithmetic: 9.84 us -> 1.03 us  [the longest x1 0.98 us: collected(): bias_grad = jnp.sum(dact_table, axis=1)]
    psum x0 -> x1, blocking collectives: none -> 8.19 us  [collected(): lax.psum(jnp.stack([picked_row(scores, hit_a), picked_row(scores, hit_b)]...]
    pallas_call x3, Pallas kernels: 295 us -> 288 us  [gathered(): pl.pallas_call(functools.partial(gather_kernel, n, tag is not None), out_...]
    convert_element_type x1 -> x2, other arithmetic: 7.2 us -> 1.44 us  [the longest x1 1.42 us: collected(): acts = (jnp.where(local_a[:, :, None] == atoms, act_a[:, :, None], 0.0) +...]
    dot_general x3, matrix products: 30.2 us -> 25.1 us  [the longest x1 11.7 us: collected(): lax.dot_general(encoder, centered_all, contract, preferred_element_type=w...]
    slice x2 -> x7, local copies, waits for them, and re-layouts: 0.18 us -> 5.05 us  [the longest x2 1.82 us: collected(): first_ids, second_ids = (ids_all[:, 0::2, :], ids_all[:, 1::2, :])]
  transfers between devices with their start and end apart: 3 -> 1, of which waited for: 1 -> 0; matrix products, arithmetic and copies ran while one was open for 3% -> 13% of each run, Pallas kernels for 22% -> 76%
where the time goes in v2:
time: 391 us
  Pallas kernels  297 us (76%)
  matrix products  43.6 us (11%)
  local copies, waits for them, and re-layouts  15.4 us (4%)
  between operations  15 us (4%)
  blocking collectives  13.2 us (3%)
  other arithmetic  6.73 us (2%)
    pallas_call x3, Pallas kernels, gathered(): pl.pallas_call(functools.partial(gather_kernel, n, tag is not None), out_...  288 us
    dot_general x1, matrix products, collected(): lax.dot_general(residual, decoder_all.reshape(owner_total * atom_dev, wid...  12.8 us
    dot_general x1, matrix products, collected(): lax.dot_general(encoder, centered_all, contract, preferred_element_type=w...  11.7 us
    dot_general x1, matrix products, collected(): jnp.dot(dact_low, centered_all, preferred_element_type=wide)  9.56 us
    pallas_call x1, Pallas kernels, decode(): pl.pallas_call(decode_kernel, grid=(n,), out_shape=jax.ShapeDtypeStruct(t...  8.33 us
    psum x1, blocking collectives, collected(): lax.psum(jnp.stack([picked_row(scores, hit_a), picked_row(scores, hit_b)]...  8.19 us
  transfers between devices with their start and end apart: 1, of which 0 were waited for; matrix products, arithmetic and copies ran while one was open for 13% of the time, Pallas kernels for 76%

profile of v2, /device:TPU:0, one launch (start us, length us, event | category | flops | bytes accessed | tf_op | source)
XLA Modules:
  0.0 390.5 jit_solution(14217485026932611520)
XLA Ops:
  7.2 0.0 copy-start
  7.2 0.0 all-reduce.2.cloned.1.call-start
  7.2 2.7 fusion.27
  9.9 0.0 all-reduce.2.cloned.1.call-update
  9.9 2.4 subtract_convert_fusion.refs_0_
  12.3 0.0 copy-start.2
  12.3 0.0 copy-start.3
  12.3 97.4 %gather_1.1 = (bf16[16,128,4096]{2,1,0:T(8,128)(2,1)}, s32[16,16,128]{2,1,0:T(8,128)}) custom-call(bf16[128,4096]{1,0:T(8,128)(2,1)} %subtract_convert_fusion.refs_0_, s32[16,128]{1,0:T(8,128)} %bitcast.120), custom_call_target="tpu_custom_call" | custom-call | bytes 134217728 | tf_op jit(solution)/shard_map/gather_1/pallas_call | solution.py:320
  109.8 0.9 slice.73
  110.7 0.9 slice.74
  111.6 0.7 slice.72
  112.3 0.7 slice.75
  113.0 1.0 slice_bitcast_fusion.15
  114.0 0.1 select_reduce_fusion.24
  114.2 0.0 copy-done
  114.2 11.7 %select_reduce_fusion.19 = (f32[2048]{0:T(1024)S(1)}, f32[2048]{0:T(1024)S(1)}, f32[2048]{0:T(1024)S(1)}, f32[2048]{0:T(1024)S(1)}) fusion(s32[2048]{0:T(1024)S(1)} %bitcast.121, s32[2048]{0:T(1024)S(1)} %bitcast.123, f32[128]{0:T(128)} %param.10, bf16[2048,4096]{1,0:T(8,128)(2,1)} %bitcast.117, bf16[128,4096]{1,0:T(8,128)(2,1)S(1)} %copy-done), kind=kOutput, calls=%fused_computation.49 | convolution fusion | flops 2150096896 | bytes 17875456 | tf_op jit(solution)/shard_map/dot_general | solution.py:395
  125.9 8.2 %psum.21 = f32[2,2048]{1,0:T(2,128)S(1)} all-reduce(f32[2,2048]{1,0:T(2,128)S(1)} %pad_maximum_fusion), channel_id=1, replica_groups=mesh['atoms'=16,'width'=2] {'width'}, use_global_device_ids=true, to_apply=%region_5.6 | all-reduce | flops 4096 | bytes 32768 | tf_op jit(solution)/shard_map/psum | solution.py:413
  134.1 0.6 reshape.102.refs_1_
  134.7 94.2 %gather_2.1 = (bf16[16,128,4096]{2,1,0:T(8,128)(2,1)}, f32[16,32,128]{2,1,0:T(8,128)}) custom-call(bf16[128,4096]{1,0:T(8,128)(2,1)} %refs_0_.1, f32[32,128]{1,0:T(8,128)} %reshape.102.refs_1_), custom_call_target="tpu_custom_call" | custom-call | bytes 134217728 | tf_op jit(solution)/shard_map/gather_2/pallas_call | solution.py:320
  229.0 0.9 constant_dynamic-slice_fusion.1
  229.9 0.1 select_reduce_fusion.25
  229.9 1.4 add_convert_fusion.1.act_ref
  231.3 0.0 copy-done.2
  231.4 0.0 copy-done.3
  231.4 0.0 copy-start.1
  231.4 5.8 %copy-done.1 = bf16[16,128,4096]{2,1,0:T(8,128)(2,1)S(1)} copy-done((bf16[16,128,4096]{2,1,0:T(8,128)(2,1)S(1)}, bf16[16,128,4096]{2,1,0:T(8,128)(2,1)}, u32[]{:S(2)}) %copy-start.1) | copy-done | bytes 16777240
  237.1 8.3 %decode.1.refs_0_ = bf16[128,4096]{1,0:T(8,128)(2,1)} custom-call(bf16[16,128,128]{2,1,0:T(8,128)(2,1)S(1)} %add_convert_fusion.1.act_ref, bf16[16,128,4096]{2,1,0:T(8,128)(2,1)S(1)} %copy-done.1, bf16[128,4096]{1,0:T(8,128)(2,1)S(1)} %copy-done.2, f32[1,4096]{1,0:T(1,128)S(1)} %bitcast.116), custom_call_target="tpu_custom_call" | custom-call | tf_op jit(solution)/shard_map/decode/pallas_call | solution.py:365
  245.5 12.8 %select_reduce_fusion = (f32[128]{0:T(128)S(1)}, f32[128]{0:T(128)S(1)}, f32[128]{0:T(128)S(1)}, f32[128]{0:T(128)S(1)}, f32[128]{0:T(128)S(1)}, /*index=5*/f32[...) fusion(s32[128]{0:T(128)S(1)} %get-tuple-element.64, ...), kind=kOutput, calls=%fused_computation.11 | convolution fusion | flops 2160066560 | bytes 17842176 | tf_op jit(solution)/shard_map/dot_general | solution.py:432
  258.2 0.1 stack.91
  258.3 5.0 %psum.22 = f32[16,128]{1,0:T(8,128)S(1)} all-reduce(f32[16,128]{1,0:T(8,128)S(1)} %stack.91), channel_id=1, replica_groups=mesh['atoms'=16,'width'=2] {'width'}, use_global_device_ids=true, to_apply=%region_25.26 | all-reduce | flops 2048 | bytes 16384 | tf_op jit(solution)/shard_map/psum | solution.py:442
  263.3 0.6 broadcast_multiply_fusion.refs_1_
  263.9 96.6 %gather_3.1 = (bf16[16,128,4096]{2,1,0:T(8,128)(2,1)}, f32[16,16,128]{2,1,0:T(8,128)}) custom-call(bf16[128,4096]{1,0:T(8,128)(2,1)} %decode.1.refs_0_, f32[16,128]{1,0:T(8,128)} %broadcast_multiply_fusion.refs_1_), custom_call_target="tpu_custom_call" | custom-call | bytes 134217728 | tf_op jit(solution)/shard_map/gather_3/pallas_call | solution.py:320
  360.5 0.9 slice.92
  361.5 0.9 slice.93
  362.4 0.0 copy-start.4
  362.4 1.0 fusion.1
  363.4 9.6 %convolution_convert_fusion = bf16[128,4096]{1,0:T(8,128)(2,1)} fusion(bf16[128,2048]{1,0:T(8,128)(2,1)S(1)} %get-tuple-element.46, bf16[2048,4096]{1,0:T(8,128)(2,1)} %bitcast.118), kind=kOutput, calls=%fused_computation.3 | convolution fusion | flops 2148007936 | bytes 18350080 | tf_op jit(solution)/shard_map/dot_general | solution.py:450
  373.0 0.0 copy-start.5
  373.7 0.0 copy-done.4
  373.7 3.8 convolution_multiply_fusion
  377.6 0.0 all-reduce.2.cloned.1.call-done
  377.6 1.9 gather_fusion
  379.5 1.0 multiply_reduce_fusion
  380.6 0.0 copy-done.5
  380.6 3.1 fusion
  (9 shorter events, 0.1 us)
Async XLA Ops:
  7.2 107.0 %copy-start = (bf16[128,4096]{1,0:T(8,128)(2,1)S(1)}, bf16[128,4096]{1,0:T(8,128)(2,1)}, u32[]{:S(2)}) copy-start(bf16[128,4096]{1,0:T(8,128)(2,1)} %param.9) | copy-start | bytes 3145732
  7.2 370.4 %all-reduce.2.cloned.1.call-start = ((), (), s32[]{:S(2)}) async-start(), calls=%async_computation | async-start | bytes 131072 | tf_op jit(solution)/shard_map/psum | solution.py:392
  12.3 219.0 %copy-start.2 = (bf16[128,4096]{1,0:T(8,128)(2,1)S(1)}, bf16[128,4096]{1,0:T(8,128)(2,1)}, u32[]{:S(2)}) copy-start(bf16[128,4096]{1,0:T(8,128)(2,1)} %tok_ref.1) | copy-start | bytes 3145732
  12.3 219.0 %copy-start.3 = (f32[4096]{0:T(1024)S(1)}, f32[4096]{0:T(1024)}, u32[]{:S(2)}) copy-start(f32[4096]{0:T(1024)} %param.8) | copy-start | bytes 49156
  231.4 5.8 %copy-start.1 = (bf16[16,128,4096]{2,1,0:T(8,128)(2,1)S(1)}, bf16[16,128,4096]{2,1,0:T(8,128)(2,1)}, u32[]{:S(2)}) copy-start(bf16[16,128,4096]{2,1,0:T(8,128)(2,1)} %get-tuple-element.13.dec_ref) | copy-start | bytes 50331652
  362.4 11.4 %copy-start.4 = (bf16[16,128,4096]{2,1,0:T(8,128)(2,1)S(1)}, bf16[16,128,4096]{2,1,0:T(8,128)(2,1)}, u32[]{:S(2)}) copy-start(bf16[16,128,4096]{2,1,0:T(8,128)(2,1)} %get-tuple-element.15) | copy-start | bytes 50331652
  373.0 7.6 %copy-start.5 = (bf16[128,4096]{1,0:T(8,128)(2,1)S(1)}, bf16[128,4096]{1,0:T(8,128)(2,1)}, u32[]{:S(2)}) copy-start(bf16[128,4096]{1,0:T(8,128)(2,1)} %refs_0_.1) | copy-start | bytes 3145732
Sparse Core Ops, SparseCore 0:
  10.3 23.4 all-reduce.1
